TPU v7x, 32 devices: a whole 2x2x4 slice. The times are simulated.
32 devices in a mesh: dp: 8 (over y, x, core), mp: 4 (over z).
Axes of the slice: x: 2, y: 2, z: 4, core: 2. Of those that a mesh axis runs over, the one named last changes fastest.
Arguments:
- token_factors: bfloat16 [4, 16384, 128], P('mp', 'dp'), may hold values from -6 to 6
- example_ids: int32 [8, 2048], P('dp'), may hold values from 0 to 7, never falling along the last dimension, each value on 1 to 1024 neighbouring positions
- left_factor: bfloat16 [4, 64, 64], P('mp'), may hold values from -0.75 to 0.75
- right_factor: bfloat16 [4, 64, 64], P('mp'), may hold values from -0.75 to 0.75
- query_features: bfloat16 [768, 16384], P('dp', 'mp'), may hold values from -0.375 to 0.375
Outputs:
- influence: float32 [768, 64], P(('dp', 'mp'))
Inputs may be any that keep to these rules, and one draw needn't show every extreme that they name: `example_ids`: each row is non-decreasing, and every example 0 to 7 has 1 to 1024 tokens in each block.
All inputs are finite; a program needn't handle non-finite values.
Results may differ from a plain program's by a relative error of at most 0.0029.
Values may be sent and summed in bfloat16 or wider, within the bound.
A program may use at most 64 MiB of HBM per device.

v0:
```python
import functools

import jax
import jax.numpy as jnp
from jax import lax
from jax.experimental import pallas as pl
from jax.experimental.pallas import tpu as pltpu
from jax.sharding import PartitionSpec as P

EX_DEV = 8
LANES = 128
F32, BF16 = jnp.float32, jnp.bfloat16
NT = (((1,), (1,)), ((), ()))


def flipped(index, mask):
    bit = 1
    while bit <= mask:
        if mask & bit:
            index = index + bit - 2 * bit * ((index // bit) % 2)
        bit *= 2
    return index


def partner(index, offset, count):
    if count & (count - 1) == 0:
        return flipped(index, offset)
    return (index + offset) % count


def iota(shape, dim):
    return lax.broadcasted_iota(jnp.int32, shape, dim)


def split(value):
    high = value.astype(BF16)
    return high, (value - high.astype(F32)).astype(BF16)


def kernel(
    n_dp, n_mp,
    tokens_hbm, ids_hbm, left_hbm, right_hbm, query_hbm, out_ref,
    tok, ids_ref, left_ref, right_ref, blocks, pscr, qbuf, fsend, fall, part, prec,
    in_sem, q_sem, qx_send, qx_recv, f_send, f_recv, p_send, p_recv,
):
    d, m = lax.axis_index("dp"), lax.axis_index("mp")
    core = d % 2
    sibling = flipped(d, 1)
    tokens = tok.shape[0]
    rank = left_ref.shape[0]
    rows_q = query_hbm.shape[0]
    half = query_hbm.shape[1] // 2
    quarter = half // 2
    rows_out = rows_q // n_mp
    groups = 2 * n_mp

    loads = []
    for i, (source, target) in enumerate(
        ((tokens_hbm.at[0], tok), (ids_hbm, ids_ref), (left_hbm.at[0], left_ref), (right_hbm.at[0], right_ref))
    ):
        loads.append(pltpu.make_async_copy(source, target, in_sem.at[i]))
        loads[-1].start()

    barrier = pltpu.get_barrier_semaphore()
    for k in range(1, n_dp):
        pl.semaphore_signal(barrier, inc=1, device_id={"dp": partner(d, k, n_dp), "mp": m})
    for k in range(1, n_mp):
        for s in range(2):
            pl.semaphore_signal(
                barrier, inc=1, device_id={"dp": flipped(d, s), "mp": partner(m, k, n_mp)}
            )

    def half_of(which):
        return pl.ds(pl.multiple_of(which * half, LANES), half)

    my_rows = pl.ds(pl.multiple_of(core * rows_q, 16), rows_q)
    load_query = pltpu.make_async_copy(query_hbm.at[:, half_of(core)], qbuf.at[my_rows], q_sem)
    load_query.start()

    loads[1].wait()
    ids = ids_ref[...]
    one, zero = jnp.ones((rank, tokens), BF16), jnp.zeros((rank, tokens), BF16)
    by_low = jnp.concatenate([jnp.where(ids % 2 == i, one, zero) for i in range(2)], axis=0)
    by_high = jnp.concatenate([jnp.where(ids // 2 == j, one, zero) for j in range(4)], axis=0)
    counts = lax.dot_general(by_low, by_high, NT, preferred_element_type=F32)

    loads[2].wait()
    loads[3].wait()
    tall = 2 * rank
    widen = (iota((rank, tall), 1) % rank == iota((rank, tall), 0)).astype(BF16)
    rows = (
        iota((tall, rank), 1) == 2 * (iota((tall, rank), 0) % (rank // 2)) + iota((tall, rank), 0) // rank
    ).astype(BF16)
    left = jnp.dot(left_ref[...], widen, preferred_element_type=F32).astype(BF16)
    left = jnp.dot(rows, left, preferred_element_type=F32)
    same = iota((tall, tall), 1) // rank == (iota((tall, tall), 0) // (rank // 2)) % 2
    left = jnp.where(same, left, 0.0).astype(BF16)
    left = jnp.concatenate([left, left], axis=1)
    wide = EX_DEV * rank
    widest = (iota((rank, wide), 1) % rank == iota((rank, wide), 0)).astype(BF16)
    right = jnp.dot(right_ref[...], widest, preferred_element_type=F32)
    column = iota((rank, wide), 1) // rank
    for p in range(2):
        for j in range(4):
            at = (p * 4 + j) * rank
            blocks[at:at + rank, :] = jnp.where(column == 2 * j + p, right, 0.0).astype(BF16)

    turn = (iota((tall, tall), 1) == iota((tall, tall), 0)).astype(BF16)
    loads[0].wait()
    turned = lax.dot_general(turn, tok[...], NT, preferred_element_type=F32).astype(BF16)
    inputs, outputs = turned[:rank], turned[rank:]
    lhs = jnp.concatenate([outputs] * 2, axis=0) * by_low
    rhs = jnp.concatenate([inputs] * 4, axis=0) * by_high
    grad = lax.dot_general(lhs, rhs, NT, preferred_element_type=F32) / counts
    high, low = split(grad)
    mixed = jnp.dot(left, jnp.concatenate([high, low], axis=0), preferred_element_type=F32)
    high, low = split(jnp.concatenate([mixed[:rank], mixed[rank:]], axis=1))
    both = jnp.dot(jnp.concatenate([high, low], axis=0), blocks[...], preferred_element_type=F32)
    precond = both[:rank] + both[rank:]
    for j in range(4):
        pscr[j * rank:(j + 1) * rank, :] = precond[:, j * LANES:(j + 1) * LANES]
    spread = rank // 2
    tiles = spread // 4
    for h in range(2):
        for j in range(tiles):
            two = [
                pscr[pl.ds((h * 2 + q) * tiles + j, EX_DEV, stride=spread), :] for q in range(2)
            ]
            fsend[h, :, j * LANES:(j + 1) * LANES] = jnp.concatenate(two, axis=0).astype(BF16)

    pl.semaphore_wait(barrier, n_dp - 1 + 2 * (n_mp - 1))

    copies = []
    for k in range(n_dp - 1, 0, -1):
        to = partner(d, k, n_dp)
        copy = pltpu.make_async_remote_copy(
            src_ref=fsend.at[to % 2],
            dst_ref=fall.at[d],
            send_sem=f_send.at[to],
            recv_sem=f_recv.at[d],
            device_id={"dp": to, "mp": m},
            device_id_type=pl.DeviceIdType.MESH,
        )
        copy.start()
        copies.append((to, copy))
    query_copy = pltpu.make_async_remote_copy(
        src_ref=query_hbm.at[:, half_of(1 - core)],
        dst_ref=qbuf.at[my_rows],
        send_sem=qx_send,
        recv_sem=qx_recv,
        device_id={"dp": sibling, "mp": m},
        device_id_type=pl.DeviceIdType.MESH,
    )
    query_copy.start()
    fall[d] = fsend[core]

    load_query.wait()
    their_rows = pl.ds(pl.multiple_of((1 - core) * rows_q, 16), rows_q)
    pltpu.make_async_remote_copy(
        src_ref=query_hbm.at[:, half_of(1 - core)],
        dst_ref=qbuf.at[their_rows],
        send_sem=qx_send,
        recv_sem=qx_recv,
        device_id={"dp": sibling, "mp": m},
        device_id_type=pl.DeviceIdType.MESH,
    ).wait_recv()
    for k in range(1, n_dp):
        source = partner(d, k, n_dp) if n_dp & (n_dp - 1) == 0 else (d + n_dp - k) % n_dp
        pltpu.make_async_remote_copy(
            src_ref=fsend.at[0],
            dst_ref=fall.at[source],
            send_sem=f_send.at[source],
            recv_sem=f_recv.at[source],
            device_id={"dp": source, "mp": m},
            device_id_type=pl.DeviceIdType.MESH,
        ).wait_recv()

    feats = fall[...].reshape(n_dp * 2 * EX_DEV, quarter)
    score = []
    for q in range(2):
        score.append(
            lax.dot_general(
                feats, qbuf[:, q * quarter:(q + 1) * quarter], NT, preferred_element_type=F32
            ).reshape(n_dp, 2, EX_DEV, 2 * rows_q)[:, q]
        )
    scores = (score[0] + score[1]).reshape(n_dp * EX_DEV, 2 * rows_q).T
    part[...] = scores.reshape(groups, rows_out, n_dp * EX_DEV)

    mine = core * n_mp + m
    sent = []
    for k in range(n_mp):
        for s in range(2):
            if k == 0 and s == 0:
                continue
            to_m = partner(m, k, n_mp)
            to_core = flipped(core, s)
            slot = to_core * n_mp + to_m
            copy = pltpu.make_async_remote_copy(
                src_ref=part.at[slot],
                dst_ref=prec.at[mine],
                send_sem=p_send.at[slot],
                recv_sem=p_recv.at[mine],
                device_id={"dp": flipped(d, s), "mp": to_m},
                device_id_type=pl.DeviceIdType.MESH,
            )
            copy.start()
            sent.append(copy)
    total = part[mine]
    for k in range(n_mp):
        for s in range(2):
            if k == 0 and s == 0:
                continue
            from_m = partner(m, k, n_mp) if n_mp & (n_mp - 1) == 0 else (m + n_mp - k) % n_mp
            slot = flipped(core, s) * n_mp + from_m
            pltpu.make_async_remote_copy(
                src_ref=part.at[slot],
                dst_ref=prec.at[slot],
                send_sem=p_send.at[slot],
                recv_sem=p_recv.at[slot],
                device_id={"dp": flipped(d, s), "mp": from_m},
                device_id_type=pl.DeviceIdType.MESH,
            ).wait_recv()
            total = total + prec[slot]
    out_ref[...] = total
    for to, copy in copies:
        copy.wait_send()
    query_copy.wait_send()
    for copy in sent:
        copy.wait_send()


def shards(n_dp, n_mp, token_factors, example_ids, left_factor, right_factor, query_features):
    tokens, rank = token_factors.shape[1], left_factor.shape[1]
    rows_q, feat = query_features.shape
    rows_out = rows_q // n_mp
    groups = 2 * n_mp
    train = n_dp * EX_DEV
    dma = pltpu.SemaphoreType.DMA
    vmem = pl.BlockSpec(memory_space=pltpu.VMEM)
    in_hbm = pl.BlockSpec(memory_space=pltpu.HBM)
    return pl.pallas_call(
        functools.partial(kernel, n_dp, n_mp),
        out_shape=jax.ShapeDtypeStruct((rows_out, train), F32),
        in_specs=[in_hbm] * 5,
        out_specs=vmem,
        scratch_shapes=[
            pltpu.VMEM((tokens, 2 * rank), BF16),
            pltpu.VMEM((1, tokens), jnp.int32),
            pltpu.VMEM((rank, rank), BF16),
            pltpu.VMEM((rank, rank), BF16),
            pltpu.VMEM((EX_DEV * rank, EX_DEV * rank), BF16),
            pltpu.VMEM((4 * rank, 2 * rank), F32),
            pltpu.VMEM((2 * rows_q, feat // 2), BF16),
            pltpu.VMEM((2, 2 * EX_DEV, feat // 4), BF16),
            pltpu.VMEM((n_dp, 2 * EX_DEV, feat // 4), BF16),
            pltpu.VMEM((groups, rows_out, train), F32),
            pltpu.VMEM((groups, rows_out, train), F32),
            dma((4,)), dma, dma, dma,
            dma((n_dp,)), dma((n_dp,)),
            dma((groups,)), dma((groups,)),
        ],
        compiler_params=pltpu.CompilerParams(
            collective_id=0, has_side_effects=True, vmem_limit_bytes=56 * 1024 * 1024
        ),
        cost_estimate=pl.CostEstimate(
            flops=2 * rank * EX_DEV * tokens * 2 * rank, bytes_accessed=2 * rows_q * feat,
            transcendentals=0,
        ),
    )(token_factors, example_ids, left_factor, right_factor, query_features)


def solution(mesh):
    placed = (
        P("mp", "dp", None),
        P("dp", None),
        P("mp", None, None),
        P("mp", None, None),
        P("dp", "mp"),
    )
    return jax.shard_map(
        functools.partial(shards, mesh.shape["dp"], mesh.shape["mp"]),
        mesh=mesh, in_specs=placed, out_specs=P(("dp", "mp"), None), check_vma=False,
    )
```

profile of v0, /device:TPU:0, one launch (start us, length us, event | category | flops | bytes accessed | tf_op | source)
XLA Modules:
  0.0 18.5 jit_solution(10218779087825273214)
XLA Ops:
  0.0 17.2 %shard_map.55 = f32[24,64]{1,0:T(8,128)} custom-call(bf16[1,2048,128]{2,1,0:T(8,128)(2,1)} %tokens_hbm.1, s32[1,2048]{1,0:T(1,128)} %ids_hbm.1, bf16[1,64,64]{2,1,0:T(8,128)(2,1)} %left_hbm.1, bf16[1,64,64]{2,1,0:T(8,128)(2,1)} %right_hbm.1, bf16[96,4096]{1,0:T(8,128)(2,1)} %query_hbm.1), custom_call_target="tpu_custom_call" | custom-call | flops 268435456 | bytes 786432 | tf_op jit(solution)/shard_map/pallas_call | solution.py:241
  17.2 1.3 %copy.7 = f32[24,64]{1,0:T(8,128)} copy(f32[24,64]{1,0:T(8,128)} %shard_map.55) | data formatting | bytes 12288
where the time goes:
time: 18.7 us; the launch traced here: 18.5 us
  Pallas kernels  17.2 us (92%)
  local copies, waits for them, and re-layouts  1.31 us (7%)
    pallas_call x1, Pallas kernels, shards(): pl.pallas_call(functools.partial(kernel, n_dp, n_mp), out_shape=jax.Shape...  17.2 us
    unnamed x1, local copies, waits for them, and re-layouts  1.31 us

commit v1 on v0

--- a/solution.py
+++ b/solution.py
@@ -77,16 +77,48 @@
     load_query = pltpu.make_async_copy(query_hbm.at[:, half_of(core)], qbuf.at[my_rows], q_sem)
     load_query.start()
 
-    loads[1].wait()
+    for load in loads:
+        load.wait()
+    pl.semaphore_wait(barrier, n_dp - 1 + 2 * (n_mp - 1))
+
+    query_copy = pltpu.make_async_remote_copy(
+        src_ref=query_hbm.at[:, half_of(1 - core)],
+        dst_ref=qbuf.at[my_rows],
+        send_sem=qx_send,
+        recv_sem=qx_recv,
+        device_id={"dp": sibling, "mp": m},
+        device_id_type=pl.DeviceIdType.MESH,
+    )
+    query_copy.start()
+
+    tall, wide = 2 * rank, EX_DEV * rank
     ids = ids_ref[...]
-    one, zero = jnp.ones((rank, tokens), BF16), jnp.zeros((rank, tokens), BF16)
-    by_low = jnp.concatenate([jnp.where(ids % 2 == i, one, zero) for i in range(2)], axis=0)
-    by_high = jnp.concatenate([jnp.where(ids // 2 == j, one, zero) for j in range(4)], axis=0)
-    counts = lax.dot_general(by_low, by_high, NT, preferred_element_type=F32)
-
-    loads[2].wait()
-    loads[3].wait()
-    tall = 2 * rank
+    member = (ids == iota((EX_DEV, tokens), 0)).astype(F32)
+    inverse = 1.0 / jnp.sum(member, axis=1, keepdims=True)
+    group = iota((1, 4 * rank), 1) // rank
+    scale = []
+    for i in range(2):
+        row = jnp.zeros((1, 4 * rank), F32)
+        for j in range(4):
+            row = jnp.where(group == j, inverse[2 * j + i:2 * j + i + 1, :], row)
+        scale.append(jnp.broadcast_to(row, (rank, 4 * rank)))
+    scale = jnp.concatenate(scale, axis=0)
+
+    step = 512
+    turn = (iota((tall, tall), 1) == iota((tall, tall), 0)).astype(BF16)
+    none = jnp.zeros((rank, step), BF16)
+    summed = jnp.zeros((tall, 4 * rank), F32)
+    for start in range(0, tokens, step):
+        turned = lax.dot_general(
+            turn, tok[start:start + step, :], NT, preferred_element_type=F32
+        ).astype(BF16)
+        inputs, outputs = turned[:rank], turned[rank:]
+        here = ids[:, start:start + step]
+        lhs = jnp.concatenate([jnp.where(here % 2 == i, outputs, none) for i in range(2)], axis=0)
+        rhs = jnp.concatenate([jnp.where(here // 2 == j, inputs, none) for j in range(4)], axis=0)
+        summed = summed + lax.dot_general(lhs, rhs, NT, preferred_element_type=F32)
+    grad = summed * scale
+
     widen = (iota((rank, tall), 1) % rank == iota((rank, tall), 0)).astype(BF16)
     rows = (
         iota((tall, rank), 1) == 2 * (iota((tall, rank), 0) % (rank // 2)) + iota((tall, rank), 0) // rank
@@ -96,7 +128,6 @@
     same = iota((tall, tall), 1) // rank == (iota((tall, tall), 0) // (rank // 2)) % 2
     left = jnp.where(same, left, 0.0).astype(BF16)
     left = jnp.concatenate([left, left], axis=1)
-    wide = EX_DEV * rank
     widest = (iota((rank, wide), 1) % rank == iota((rank, wide), 0)).astype(BF16)
     right = jnp.dot(right_ref[...], widest, preferred_element_type=F32)
     column = iota((rank, wide), 1) // rank
@@ -105,13 +136,6 @@
             at = (p * 4 + j) * rank
             blocks[at:at + rank, :] = jnp.where(column == 2 * j + p, right, 0.0).astype(BF16)
 
-    turn = (iota((tall, tall), 1) == iota((tall, tall), 0)).astype(BF16)
-    loads[0].wait()
-    turned = lax.dot_general(turn, tok[...], NT, preferred_element_type=F32).astype(BF16)
-    inputs, outputs = turned[:rank], turned[rank:]
-    lhs = jnp.concatenate([outputs] * 2, axis=0) * by_low
-    rhs = jnp.concatenate([inputs] * 4, axis=0) * by_high
-    grad = lax.dot_general(lhs, rhs, NT, preferred_element_type=F32) / counts
     high, low = split(grad)
     mixed = jnp.dot(left, jnp.concatenate([high, low], axis=0), preferred_element_type=F32)
     high, low = split(jnp.concatenate([mixed[:rank], mixed[rank:]], axis=1))
@@ -128,8 +152,6 @@
             ]
             fsend[h, :, j * LANES:(j + 1) * LANES] = jnp.concatenate(two, axis=0).astype(BF16)
 
-    pl.semaphore_wait(barrier, n_dp - 1 + 2 * (n_mp - 1))
-
     copies = []
     for k in range(n_dp - 1, 0, -1):
         to = partner(d, k, n_dp)
@@ -143,15 +165,6 @@
         )
         copy.start()
         copies.append((to, copy))
-    query_copy = pltpu.make_async_remote_copy(
-        src_ref=query_hbm.at[:, half_of(1 - core)],
-        dst_ref=qbuf.at[my_rows],
-        send_sem=qx_send,
-        recv_sem=qx_recv,
-        device_id={"dp": sibling, "mp": m},
-        device_id_type=pl.DeviceIdType.MESH,
-    )
-    query_copy.start()
     fall[d] = fsend[core]
 
     load_query.wait()
@@ -240,7 +253,7 @@
     in_hbm = pl.BlockSpec(memory_space=pltpu.HBM)
     return pl.pallas_call(
         functools.partial(kernel, n_dp, n_mp),
-        out_shape=jax.ShapeDtypeStruct((rows_out, train), F32),
+        out_shape=pltpu.VMEM((rows_out, train), F32),
         in_specs=[in_hbm] * 5,
         out_specs=vmem,
         scratch_shapes=[
@@ -260,13 +273,16 @@
             dma((groups,)), dma((groups,)),
         ],
         compiler_params=pltpu.CompilerParams(
-            collective_id=0, has_side_effects=True, vmem_limit_bytes=56 * 1024 * 1024
+            collective_id=0, has_side_effects=True, vmem_limit_bytes=16 * 1024 * 1024
         ),
         cost_estimate=pl.CostEstimate(
             flops=2 * rank * EX_DEV * tokens * 2 * rank, bytes_accessed=2 * rows_q * feat,
             transcendentals=0,
         ),
-    )(token_factors, example_ids, left_factor, right_factor, query_features)
+    )(*(
+        pltpu.with_memory_space_constraint(array, pltpu.HBM)
+        for array in (token_factors, example_ids, left_factor, right_factor, query_features)
+    ))
 
 
 def solution(mesh):

time: 18.7 us -> 17 us (0.909)
  Pallas kernels: 17.2 us -> 16.3 us
  local copies, waits for them, and re-layouts: 1.31 us -> 0.6 us
    pallas_call x1, Pallas kernels: 17.2 us -> 16.3 us  [shards(): pl.pallas_call(functools.partial(kernel, n_dp, n_mp), out_shape=pltpu.VME...]
    unnamed x1, local copies, waits for them, and re-layouts: 1.31 us -> 0.6 us
where the time goes in v1:
time: 17 us; the launch traced here: 16.9 us
  Pallas kernels  16.3 us (96%)
  local copies, waits for them, and re-layouts  0.6 us (4%)
    pallas_call x1, Pallas kernels, shards(): pl.pallas_call(functools.partial(kernel, n_dp, n_mp), out_shape=pltpu.VME...  16.3 us
    unnamed x1, local copies, waits for them, and re-layouts  0.6 us

profile of v1, /device:TPU:0, one launch (start us, length us, event | category | flops | bytes accessed | tf_op | source)
XLA Modules:
  0.0 16.9 jit_solution(1411654466352447917)
XLA Ops:
  0.0 16.3 %shard_map.55 = f32[24,64]{1,0:T(8,128)S(1)} custom-call(bf16[1,2048,128]{2,1,0:T(8,128)(2,1)} %tokens_hbm.1, s32[1,2048]{1,0:T(1,128)} %ids_hbm.1, bf16[1,64,64]{2,1,0:T(8,128)(2,1)} %left_hbm.1, bf16[1,64,64]{2,1,0:T(8,128)(2,1)} %right_hbm.1, bf16[96,4096]{1,0:T(8,128)(2,1)} %query_hbm.1), custom_call_target="tpu_custom_call" | custom-call | flops 268435456 | bytes 786432 | tf_op jit(solution)/shard_map/pallas_call | solution.py:254
  16.3 0.6 %copy.7 = f32[24,64]{1,0:T(8,128)} copy(f32[24,64]{1,0:T(8,128)S(1)} %shard_map.55) | data formatting | bytes 12288

commit v2 on v1

--- a/solution.py
+++ b/solution.py
@@ -79,18 +79,6 @@
 
     for load in loads:
         load.wait()
-    pl.semaphore_wait(barrier, n_dp - 1 + 2 * (n_mp - 1))
-
-    query_copy = pltpu.make_async_remote_copy(
-        src_ref=query_hbm.at[:, half_of(1 - core)],
-        dst_ref=qbuf.at[my_rows],
-        send_sem=qx_send,
-        recv_sem=qx_recv,
-        device_id={"dp": sibling, "mp": m},
-        device_id_type=pl.DeviceIdType.MESH,
-    )
-    query_copy.start()
-
     tall, wide = 2 * rank, EX_DEV * rank
     ids = ids_ref[...]
     member = (ids == iota((EX_DEV, tokens), 0)).astype(F32)
@@ -152,6 +140,8 @@
             ]
             fsend[h, :, j * LANES:(j + 1) * LANES] = jnp.concatenate(two, axis=0).astype(BF16)
 
+    pl.semaphore_wait(barrier, n_dp - 1 + 2 * (n_mp - 1))
+
     copies = []
     for k in range(n_dp - 1, 0, -1):
         to = partner(d, k, n_dp)
@@ -165,18 +155,18 @@
         )
         copy.start()
         copies.append((to, copy))
-    fall[d] = fsend[core]
-
-    load_query.wait()
-    their_rows = pl.ds(pl.multiple_of((1 - core) * rows_q, 16), rows_q)
-    pltpu.make_async_remote_copy(
+    query_copy = pltpu.make_async_remote_copy(
         src_ref=query_hbm.at[:, half_of(1 - core)],
-        dst_ref=qbuf.at[their_rows],
+        dst_ref=qbuf.at[my_rows],
         send_sem=qx_send,
         recv_sem=qx_recv,
         device_id={"dp": sibling, "mp": m},
         device_id_type=pl.DeviceIdType.MESH,
-    ).wait_recv()
+    )
+    query_copy.start()
+    fall[d] = fsend[core]
+
+    load_query.wait()
     for k in range(1, n_dp):
         source = partner(d, k, n_dp) if n_dp & (n_dp - 1) == 0 else (d + n_dp - k) % n_dp
         pltpu.make_async_remote_copy(
@@ -189,24 +179,34 @@
         ).wait_recv()
 
     feats = fall[...].reshape(n_dp * 2 * EX_DEV, quarter)
-    score = []
-    for q in range(2):
-        score.append(
-            lax.dot_general(
-                feats, qbuf[:, q * quarter:(q + 1) * quarter], NT, preferred_element_type=F32
-            ).reshape(n_dp, 2, EX_DEV, 2 * rows_q)[:, q]
-        )
-    scores = (score[0] + score[1]).reshape(n_dp * EX_DEV, 2 * rows_q).T
-    part[...] = scores.reshape(groups, rows_out, n_dp * EX_DEV)
-
+    their_rows = pl.ds(pl.multiple_of((1 - core) * rows_q, 16), rows_q)
     mine = core * n_mp + m
     sent = []
-    for k in range(n_mp):
-        for s in range(2):
+    for s in range(2):
+        to_core = flipped(core, s)
+        if s == 1:
+            pltpu.make_async_remote_copy(
+                src_ref=query_hbm.at[:, half_of(1 - core)],
+                dst_ref=qbuf.at[their_rows],
+                send_sem=qx_send,
+                recv_sem=qx_recv,
+                device_id={"dp": sibling, "mp": m},
+                device_id_type=pl.DeviceIdType.MESH,
+            ).wait_recv()
+        at = their_rows if s else my_rows
+        score = []
+        for q in range(2):
+            score.append(
+                lax.dot_general(
+                    feats, qbuf[at, q * quarter:(q + 1) * quarter], NT, preferred_element_type=F32
+                ).reshape(n_dp, 2, EX_DEV, rows_q)[:, q]
+            )
+        scores = (score[0] + score[1]).reshape(n_dp * EX_DEV, rows_q).T
+        part[pl.ds(to_core * n_mp, n_mp)] = scores.reshape(n_mp, rows_out, n_dp * EX_DEV)
+        for k in range(n_mp - 1, -1, -1):
             if k == 0 and s == 0:
                 continue
             to_m = partner(m, k, n_mp)
-            to_core = flipped(core, s)
             slot = to_core * n_mp + to_m
             copy = pltpu.make_async_remote_copy(
                 src_ref=part.at[slot],

time: 17 us -> 16 us (0.941)
  Pallas kernels: 16.3 us -> 15.3 us
    pallas_call x1, Pallas kernels: 16.3 us -> 15.3 us  [shards(): pl.pallas_call(functools.partial(kernel, n_dp, n_mp), out_shape=pltpu.VME...]
where the time goes in v2:
time: 16 us; the launch traced here: 15.9 us
  Pallas kernels  15.3 us (96%)
  local copies, waits for them, and re-layouts  0.6 us (4%)
    pallas_call x1, Pallas kernels, shards(): pl.pallas_call(functools.partial(kernel, n_dp, n_mp), out_shape=pltpu.VME...  15.3 us
    unnamed x1, local copies, waits for them, and re-layouts  0.6 us

profile of v2, /device:TPU:0, one launch (start us, length us, event | category | flops | bytes accessed | tf_op | source)
XLA Modules:
  0.0 15.9 jit_solution(10571483582488817543)
XLA Ops:
  0.0 15.3 %shard_map.55 = f32[24,64]{1,0:T(8,128)S(1)} custom-call(bf16[1,2048,128]{2,1,0:T(8,128)(2,1)} %tokens_hbm.1, s32[1,2048]{1,0:T(1,128)} %ids_hbm.1, bf16[1,64,64]{2,1,0:T(8,128)(2,1)} %left_hbm.1, bf16[1,64,64]{2,1,0:T(8,128)(2,1)} %right_hbm.1, bf16[96,4096]{1,0:T(8,128)(2,1)} %query_hbm.1), custom_call_target="tpu_custom_call" | custom-call | flops 268435456 | bytes 786432 | tf_op jit(solution)/shard_map/pallas_call | solution.py:254
  15.3 0.6 %copy.7 = f32[24,64]{1,0:T(8,128)} copy(f32[24,64]{1,0:T(8,128)S(1)} %shard_map.55) | data formatting | bytes 12288

commit v3 on v2

--- a/solution.py
+++ b/solution.py
@@ -56,7 +56,7 @@
 
     loads = []
     for i, (source, target) in enumerate(
-        ((tokens_hbm.at[0], tok), (ids_hbm, ids_ref), (left_hbm.at[0], left_ref), (right_hbm.at[0], right_ref))
+        ((ids_hbm, ids_ref), (left_hbm.at[0], left_ref), (right_hbm.at[0], right_ref), (tokens_hbm.at[0], tok))
     ):
         loads.append(pltpu.make_async_copy(source, target, in_sem.at[i]))
         loads[-1].start()
@@ -77,7 +77,7 @@
     load_query = pltpu.make_async_copy(query_hbm.at[:, half_of(core)], qbuf.at[my_rows], q_sem)
     load_query.start()
 
-    for load in loads:
+    for load in loads[:3]:
         load.wait()
     tall, wide = 2 * rank, EX_DEV * rank
     ids = ids_ref[...]
@@ -91,21 +91,6 @@
             row = jnp.where(group == j, inverse[2 * j + i:2 * j + i + 1, :], row)
         scale.append(jnp.broadcast_to(row, (rank, 4 * rank)))
     scale = jnp.concatenate(scale, axis=0)
-
-    step = 512
-    turn = (iota((tall, tall), 1) == iota((tall, tall), 0)).astype(BF16)
-    none = jnp.zeros((rank, step), BF16)
-    summed = jnp.zeros((tall, 4 * rank), F32)
-    for start in range(0, tokens, step):
-        turned = lax.dot_general(
-            turn, tok[start:start + step, :], NT, preferred_element_type=F32
-        ).astype(BF16)
-        inputs, outputs = turned[:rank], turned[rank:]
-        here = ids[:, start:start + step]
-        lhs = jnp.concatenate([jnp.where(here % 2 == i, outputs, none) for i in range(2)], axis=0)
-        rhs = jnp.concatenate([jnp.where(here // 2 == j, inputs, none) for j in range(4)], axis=0)
-        summed = summed + lax.dot_general(lhs, rhs, NT, preferred_element_type=F32)
-    grad = summed * scale
 
     widen = (iota((rank, tall), 1) % rank == iota((rank, tall), 0)).astype(BF16)
     rows = (
@@ -123,6 +108,22 @@
         for j in range(4):
             at = (p * 4 + j) * rank
             blocks[at:at + rank, :] = jnp.where(column == 2 * j + p, right, 0.0).astype(BF16)
+
+    loads[3].wait()
+    step = 512
+    turn = (iota((tall, tall), 1) == iota((tall, tall), 0)).astype(BF16)
+    none = jnp.zeros((rank, step), BF16)
+    summed = jnp.zeros((tall, 4 * rank), F32)
+    for start in range(0, tokens, step):
+        turned = lax.dot_general(
+            turn, tok[start:start + step, :], NT, preferred_element_type=F32
+        ).astype(BF16)
+        inputs, outputs = turned[:rank], turned[rank:]
+        here = ids[:, start:start + step]
+        lhs = jnp.concatenate([jnp.where(here % 2 == i, outputs, none) for i in range(2)], axis=0)
+        rhs = jnp.concatenate([jnp.where(here // 2 == j, inputs, none) for j in range(4)], axis=0)
+        summed = summed + lax.dot_general(lhs, rhs, NT, preferred_element_type=F32)
+    grad = summed * scale
 
     high, low = split(grad)
     mixed = jnp.dot(left, jnp.concatenate([high, low], axis=0), preferred_element_type=F32)

time: 16 us -> 16.1 us (level)
  no operation moved by 1% of the time
where the time goes in v3:
time: 16.1 us; the launch traced here: 15.9 us
  Pallas kernels  15.3 us (95%)
  local copies, waits for them, and re-layouts  0.6 us (4%)
    pallas_call x1, Pallas kernels, shards(): pl.pallas_call(functools.partial(kernel, n_dp, n_mp), out_shape=pltpu.VME...  15.3 us
    unnamed x1, local copies, waits for them, and re-layouts  0.6 us

profile of v3, /device:TPU:0, one launch (start us, length us, event | category | flops | bytes accessed | tf_op | source)
XLA Modules:
  0.0 15.9 jit_solution(315618912391449802)
XLA Ops:
  0.0 15.3 %shard_map.55 = f32[24,64]{1,0:T(8,128)S(1)} custom-call(bf16[1,2048,128]{2,1,0:T(8,128)(2,1)} %tokens_hbm.1, s32[1,2048]{1,0:T(1,128)} %ids_hbm.1, bf16[1,64,64]{2,1,0:T(8,128)(2,1)} %left_hbm.1, bf16[1,64,64]{2,1,0:T(8,128)(2,1)} %right_hbm.1, bf16[96,4096]{1,0:T(8,128)(2,1)} %query_hbm.1), custom_call_target="tpu_custom_call" | custom-call | flops 268435456 | bytes 786432 | tf_op jit(solution)/shard_map/pallas_call | solution.py:255
  15.3 0.6 %copy.7 = f32[24,64]{1,0:T(8,128)} copy(f32[24,64]{1,0:T(8,128)S(1)} %shard_map.55) | data formatting | bytes 12288

commit v4 on v2

--- a/solution.py
+++ b/solution.py
@@ -133,18 +133,11 @@
         pscr[j * rank:(j + 1) * rank, :] = precond[:, j * LANES:(j + 1) * LANES]
     spread = rank // 2
     tiles = spread // 4
-    for h in range(2):
-        for j in range(tiles):
-            two = [
-                pscr[pl.ds((h * 2 + q) * tiles + j, EX_DEV, stride=spread), :] for q in range(2)
-            ]
-            fsend[h, :, j * LANES:(j + 1) * LANES] = jnp.concatenate(two, axis=0).astype(BF16)
-
     pl.semaphore_wait(barrier, n_dp - 1 + 2 * (n_mp - 1))
 
     copies = []
-    for k in range(n_dp - 1, 0, -1):
-        to = partner(d, k, n_dp)
+
+    def send_features(to):
         copy = pltpu.make_async_remote_copy(
             src_ref=fsend.at[to % 2],
             dst_ref=fall.at[d],
@@ -155,6 +148,17 @@
         )
         copy.start()
         copies.append((to, copy))
+
+    for h in range(2):
+        for j in range(tiles):
+            two = [
+                pscr[pl.ds((h * 2 + q) * tiles + j, EX_DEV, stride=spread), :] for q in range(2)
+            ]
+            fsend[h, :, j * LANES:(j + 1) * LANES] = jnp.concatenate(two, axis=0).astype(BF16)
+        for k in range(n_dp // 2 - 1, 0, -1):
+            send_features(2 * partner(d // 2, k, n_dp // 2) + h)
+
+    send_features(sibling)
     query_copy = pltpu.make_async_remote_copy(
         src_ref=query_hbm.at[:, half_of(1 - core)],
         dst_ref=qbuf.at[my_rows],

time: 16 us -> 16.4 us (1.025)
  Pallas kernels: 15.3 us -> 15.7 us
    pallas_call x1, Pallas kernels: 15.3 us -> 15.7 us  [shards(): pl.pallas_call(functools.partial(kernel, n_dp, n_mp), out_shape=pltpu.VME...]
where the time goes in v4:
time: 16.4 us; the launch traced here: 16.3 us
  Pallas kernels  15.7 us (96%)
  local copies, waits for them, and re-layouts  0.6 us (4%)
    pallas_call x1, Pallas kernels, shards(): pl.pallas_call(functools.partial(kernel, n_dp, n_mp), out_shape=pltpu.VME...  15.7 us
    unnamed x1, local copies, waits for them, and re-layouts  0.6 us

profile of v4, /device:TPU:0, one launch (start us, length us, event | category | flops | bytes accessed | tf_op | source)
XLA Modules:
  0.0 16.3 jit_solution(2707949762987289975)
XLA Ops:
  0.0 15.7 %shard_map.55 = f32[24,64]{1,0:T(8,128)S(1)} custom-call(bf16[1,2048,128]{2,1,0:T(8,128)(2,1)} %tokens_hbm.1, s32[1,2048]{1,0:T(1,128)} %ids_hbm.1, bf16[1,64,64]{2,1,0:T(8,128)(2,1)} %left_hbm.1, bf16[1,64,64]{2,1,0:T(8,128)(2,1)} %right_hbm.1, bf16[96,4096]{1,0:T(8,128)(2,1)} %query_hbm.1), custom_call_target="tpu_custom_call" | custom-call | flops 268435456 | bytes 786432 | tf_op jit(solution)/shard_map/pallas_call | solution.py:258
  15.7 0.6 %copy.7 = f32[24,64]{1,0:T(8,128)} copy(f32[24,64]{1,0:T(8,128)S(1)} %shard_map.55) | data formatting | bytes 12288
